TPU v7x, 32 devices: a whole 2x2x4 slice. The times are simulated.
32 devices in a mesh: gx: 4 (over x, core), gy: 8 (over z, y).
Axes of the slice: x: 2, y: 2, z: 4, core: 2. Of those that a mesh axis runs over, the one named last changes fastest.
Arguments:
- atom_feat: bfloat16 [4, 8, 32, 64], P('gx', 'gy'), may hold values from -6 to 6
- bond_feat: bfloat16 [4, 8, 32, 1024], P('gx', 'gy'), may hold values from -6 to 6
- neighbours: int32 [4, 8, 32, 16], P('gx', 'gy'), may hold values from 0 to 1023, as said below
- bond_dirs: float32 [2, 4, 8, 512], P(None, 'gx', 'gy'), may hold values from -3.140625 to 3.140625
- bond_in_weight: bfloat16 [192, 128], replicated, may hold values from -0.4375 to 0.4375
- bond_mix_weight: bfloat16 [64, 64], replicated, may hold values from -0.75 to 0.75
- pair_weight: bfloat16 [64, 256], replicated, may hold values from -0.75 to 0.75
- angle_weight: bfloat16 [64, 128], replicated, may hold values from -0.75 to 0.75
- pair_hidden_weight: bfloat16 [64, 128], replicated, may hold values from -0.75 to 0.75
- pair_out_weight: bfloat16 [64, 64], replicated, may hold values from -0.1875 to 0.1875
- atom_in_weight: bfloat16 [128, 128], replicated, may hold values from -0.5 to 0.5
- atom_out_weight: bfloat16 [64, 64], replicated, may hold values from -0.75 to 0.75
Outputs:
- atom_out: bfloat16 [4, 8, 32, 64], P('gx', 'gy')
- bond_out: bfloat16 [4, 8, 32, 1024], P('gx', 'gy')
Inputs may be any that keep to these rules, and one draw needn't show every extreme that they name: Atom neighbours[i, p] lies in atom i's block or in one of the eight blocks next to it along gx and gy, wrapping round at the ends; atom neighbours[i, p] has atom i at slot 15 - p. Every block has the same numbers of bonds pointing into each of these nine blocks, at most 64, and exactly 64 into itself.
All inputs are finite; a program needn't handle non-finite values.
Results may differ from a plain program's by a relative error of at most 0.008.
Values may be sent and summed in bfloat16 or wider, within the bound.
No kernel may reach another device: no remote copies, remote signals or barrier semaphores. Data moves between devices by JAX's collectives and lax.ppermute only.
A program may use at most 64 MiB of HBM per device.

v0:
```python
import functools

import jax
import jax.numpy as jnp
from jax import lax
from jax.experimental import pallas as pl
from jax.experimental.pallas import tpu as pltpu
from jax.sharding import PartitionSpec as P

F32 = jnp.float32
BF16 = jnp.bfloat16
CAP = 64


def quotient(values, size):
    if size & (size - 1) == 0:
        return values >> (size.bit_length() - 1)
    return lax.div(values, jnp.int32(size))


def remainder(values, size):
    if size & (size - 1) == 0:
        return values & (size - 1)
    return lax.rem(values, jnp.int32(size))


def step_code(owner, home, extent, receives):
    step = remainder(owner - home + 1 + extent, extent)
    if extent % 2 == 0:
        first = remainder(home, 2) == 0
        ahead = jnp.where(first, 2, 0)
    else:
        ahead = 0 if receives else 2
    return jnp.where(step == 1, 0, jnp.where(step == ahead, 1, 2))


def partners(extent):
    if extent % 2 == 0:
        one = [(i, i ^ 1) for i in range(extent)]
        two = [(i, ((i + 1) ^ 1) - 1) for i in range(extent)]
        two = [(i, j % extent) for i, j in two]
        return one, two
    return (
        [(i, (i + 1) % extent) for i in range(extent)],
        [((i + 1) % extent, i) for i in range(extent)],
    )


def own_rows(atom_ref, bond_ref, slots):
    atom = atom_ref[0, 0].astype(F32)
    feature = atom.shape[1]
    rows = []
    for slot in range(slots):
        bond = bond_ref[0, 0, :, slot * feature : (slot + 1) * feature].astype(F32)
        rows.append(jnp.concatenate([atom, bond], axis=1))
    return jnp.concatenate(rows, axis=0).astype(BF16)


def slot_major(table):
    slots, atoms = table.shape
    per_group = 128 // atoms
    tiled = jnp.concatenate([table.astype(F32)] * per_group, axis=1)
    row = lax.broadcasted_iota(jnp.int32, tiled.shape, 0)
    slot = quotient(lax.broadcasted_iota(jnp.int32, tiled.shape, 1), atoms)
    pieces = [
        jnp.sum(jnp.where(row == slot + group * per_group, tiled, 0.0), axis=0, keepdims=True)
        for group in range(slots // per_group)
    ]
    return jnp.concatenate(pieces, axis=1).astype(jnp.int32)


def bond_codes(targets, atoms, extents, receives):
    owner = quotient(targets, atoms)
    code_x = step_code(quotient(owner, extents[1]), lax.axis_index("gx"), extents[0], receives)
    code_y = step_code(remainder(owner, extents[1]), lax.axis_index("gy"), extents[1], receives)
    return code_x, code_y


def pack_kernel(
    extents,
    targets_hbm,
    atom_hbm,
    bond_hbm,
    own_ref,
    one_ref,
    two_ref,
    targets_ref,
    atom_ref,
    bond_ref,
    sems,
):
    copies = [
        pltpu.make_async_copy(source, target, sems.at[k])
        for k, (source, target) in enumerate(
            ((targets_hbm, targets_ref), (atom_hbm, atom_ref), (bond_hbm, bond_ref))
        )
    ]
    for copy in copies:
        copy.start()
    atoms = atom_ref.shape[2]
    slots = targets_ref.shape[0]
    bonds = slots * atoms
    lanes = 128
    groups = bonds // lanes
    copies[0].wait()
    code_x, code_y = bond_codes(slot_major(targets_ref[...]), atoms, extents, False)
    code = 3 * code_x + code_y
    rows = lax.broadcasted_iota(jnp.int32, (16, lanes), 0)
    marks = [rows == code[:, g * lanes : (g + 1) * lanes] for g in range(groups)]
    stacked = jnp.concatenate([m.astype(F32) for m in marks], axis=0).astype(BF16)
    before = lax.broadcasted_iota(jnp.int32, (lanes, 2 * lanes), 0)
    after = lax.broadcasted_iota(jnp.int32, (lanes, 2 * lanes), 1)
    sums = jnp.where((before < after) | (after >= lanes), 1.0, 0.0).astype(BF16)
    counted = jnp.dot(stacked, sums, preferred_element_type=F32)
    place = []
    earlier = jnp.zeros((16, lanes), F32)
    for g in range(groups):
        part = counted[g * 16 : (g + 1) * 16]
        place.append(
            jnp.sum(jnp.where(marks[g], part[:, :lanes] + earlier, 0.0), axis=0, keepdims=True)
        )
        earlier = earlier + part[:, lanes:]
    place = jnp.concatenate(place, axis=1).astype(jnp.int32) + CAP * code
    copies[1].wait()
    copies[2].wait()
    values = own_rows(atom_ref, bond_ref, slots)
    for third, ref in enumerate((own_ref, one_ref, two_ref)):
        spot = lax.broadcasted_iota(jnp.int32, (3 * CAP, bonds), 0) + 3 * CAP * third
        chosen = jnp.where(spot == place, 1.0, 0.0).astype(BF16)
        ref[...] = jnp.dot(chosen, values, preferred_element_type=F32).astype(BF16)


def basis_kernel(atoms, dirs_ref, basis_ref):
    slots, degrees, bonds = basis_ref.shape
    angles = dirs_ref[...]
    sines = jnp.sin(angles)
    cosines = jnp.cos(angles)
    parts = (
        sines[0:1] * cosines[1:2],
        sines[0:1] * sines[1:2],
        cosines[0:1],
    )
    unit = [jnp.broadcast_to(part, (8, bonds)) for part in parts]
    row = lax.broadcasted_iota(jnp.int32, (8, bonds), 0)
    for diagonal in range(slots):
        if diagonal == 0:
            cosine = unit[0] * unit[0] + unit[1] * unit[1] + unit[2] * unit[2]
        else:
            shift = bonds - atoms * diagonal
            turned = [pltpu.roll(part, shift, 1) for part in unit]
            cosine = unit[0] * turned[0] + unit[1] * turned[1] + unit[2] * turned[2]
        series = [jnp.ones_like(cosine), cosine]
        double = cosine + cosine
        for _ in range(7):
            series.append(double * series[-1] - series[-2])
        lower = series[7]
        upper = series[1]
        for index in range(1, 8):
            lower = jnp.where(row == index, series[7 - index], lower)
            upper = jnp.where(row == index, series[1 + index], upper)
        double = series[8] + series[8]
        blocks = [lower, upper]
        for _ in range(degrees // 8 - 1):
            blocks.append(double * blocks[-1] - blocks[-2])
        basis_ref[diagonal] = jnp.concatenate(blocks[1:], axis=0).astype(BF16)


def prepare_kernel(
    extents,
    targets_ref,
    atom_ref,
    bond_ref,
    bond_in_ref,
    bond_mix_ref,
    pair_ref,
    angle_ref,
    pair_hidden_ref,
    pair_out_ref,
    atom_in_ref,
    atom_out_ref,
    chosen_ref,
    values_ref,
    near_ref,
    far_weight_ref,
    mix_weight_ref,
    pair_weight_ref,
    angle_weight_ref,
    hidden_weight_ref,
    out_weight_ref,
    atom_in_weight_ref,
    atom_out_weight_ref,
):
    atoms = atom_ref.shape[2]
    feature = atom_ref.shape[3]
    slots = targets_ref.shape[0]
    bonds = slots * atoms
    targets = slot_major(targets_ref[...])
    code_x, code_y = bond_codes(targets, atoms, extents, True)
    code = 3 * code_y + code_x
    bond = lax.broadcasted_iota(jnp.int32, (1, bonds), 1)
    far = (slots - 1 - quotient(bond, atoms)) * atoms + remainder(targets, atoms)
    base = (code * bonds).astype(F32)
    key = base + far.astype(F32)
    column = jnp.broadcast_to(key, (128, bonds)).T
    place = []
    for group in range(bonds // 128):
        here = slice(group * 128, (group + 1) * 128)
        inside = (column < key[:, here]) & (column >= base[:, here])
        place.append(jnp.sum(jnp.where(inside, 1.0, 0.0), axis=0, keepdims=True))
    place = jnp.concatenate(place, axis=1).astype(jnp.int32) + CAP * code
    spot = lax.broadcasted_iota(jnp.int32, (9 * CAP, bonds), 0)
    chosen_ref[...] = jnp.where(spot == place, 1.0, 0.0).astype(BF16)

    values = own_rows(atom_ref, bond_ref, slots).astype(F32).T.astype(BF16)
    values_ref[...] = values

    def turned(weight, scale):
        return (weight * scale).T.astype(BF16)

    weight = bond_in_ref[...].astype(F32)
    source, other, own = (weight[k * feature : (k + 1) * feature] for k in range(3))
    empty = jnp.zeros((feature, feature), F32)

    def crossed(left, right):
        return jnp.concatenate(
            [left[:, :feature], right[:, :feature], left[:, feature:], right[:, feature:]], axis=1
        )

    blank = jnp.zeros_like(own)
    near = jnp.concatenate([crossed(source, other), crossed(own, blank)], axis=0)
    away = jnp.concatenate([crossed(other, source), crossed(blank, own)], axis=0)
    near_ref[...] = jnp.dot(turned(near, 0.5), values, preferred_element_type=F32)
    far_weight_ref[...] = turned(away, 0.5)
    mix = bond_mix_ref[...].astype(F32)
    mix = jnp.concatenate(
        [jnp.concatenate([mix, empty], axis=1), jnp.concatenate([empty, mix], axis=1)], axis=0
    )
    mix_weight_ref[...] = turned(mix, 0.5)
    pair_weight_ref[...] = turned(pair_ref[...].astype(F32), 0.5)
    angle_weight_ref[...] = turned(angle_ref[...].astype(F32), 0.5)
    hidden_weight_ref[...] = turned(pair_hidden_ref[...].astype(F32), 0.25)
    out_weight_ref[...] = turned(pair_out_ref[...].astype(F32), 0.5)
    atom_in_weight_ref[...] = turned(atom_in_ref[...].astype(F32), 0.5)
    atom_out_weight_ref[...] = turned(atom_out_ref[...].astype(F32), 0.5)


def doubled_gate(values):
    half = values.shape[0] // 2
    return values[:half] * (1.0 + jnp.tanh(values[:half])) * (1.0 + jnp.tanh(values[half:]))


def main_kernel(
    own_ref,
    one_ref,
    two_ref,
    three_ref,
    four_ref,
    basis_ref,
    chosen_ref,
    values_ref,
    near_ref,
    far_weight_ref,
    mix_weight_ref,
    pair_weight_ref,
    angle_weight_ref,
    hidden_weight_ref,
    out_weight_ref,
    atom_in_weight_ref,
    atom_out_weight_ref,
    atom_result_ref,
    bond_result_ref,
    first_ref,
    second_ref,
):
    slots, degrees, bonds = basis_ref.shape
    atoms = bonds // slots
    feature = values_ref.shape[0] // 2
    received = jnp.concatenate(
        [own_ref[0:CAP], one_ref[0:CAP], two_ref[0:CAP], three_ref[...], four_ref[...]], axis=0
    )
    received = received.astype(F32).T.astype(BF16)
    far = jnp.dot(received, chosen_ref[...], preferred_element_type=F32)
    incoming = near_ref[...] + jnp.dot(
        far_weight_ref[...], far.astype(BF16), preferred_element_type=F32
    )
    hidden = doubled_gate(incoming).astype(BF16)
    mixed = jnp.dot(mix_weight_ref[...], hidden, preferred_element_type=F32)
    ahead = (values_ref[feature:].astype(F32) + mixed[:feature]).astype(BF16).astype(F32)
    back = (far[feature:] + mixed[feature:]).astype(BF16).astype(F32)
    average = ((ahead + back) * 0.5).astype(BF16)
    projected = jnp.dot(pair_weight_ref[...], average, preferred_element_type=F32)
    first_ref[...] = projected[: 2 * feature]
    second = projected[2 * feature :]
    per_group = 128 // atoms
    for turn in range(per_group):
        second_ref[turn] = second if turn == 0 else pltpu.roll(second, bonds - atoms * turn, 1)
    width = 256
    blocks = bonds // 128
    angle_weight = angle_weight_ref[...]
    hidden_weight = hidden_weight_ref[...]
    totals = []
    for start in range(0, bonds, width):
        total = jnp.zeros((feature, width), F32)
        for diagonal in range(slots):
            turn, skip = diagonal % per_group, diagonal // per_group
            pieces = [
                second_ref[turn, :, pl.ds(128 * ((start // 128 + k + skip) % blocks), 128)]
                for k in range(width // 128)
            ]
            mixture = jnp.dot(
                angle_weight,
                basis_ref[diagonal, :, pl.ds(start, width)],
                preferred_element_type=F32,
            )
            mixture = mixture + (first_ref[:, pl.ds(start, width)] + jnp.concatenate(pieces, axis=1))
            pair = doubled_gate(mixture).astype(BF16)
            total = total + doubled_gate(
                jnp.dot(hidden_weight, pair, preferred_element_type=F32)
            )
        totals.append(total)
    pair_sum = jnp.concatenate(totals, axis=1).astype(BF16)
    bond_out = (
        average.astype(F32) + jnp.dot(out_weight_ref[...], pair_sum, preferred_element_type=F32)
    ).astype(BF16).astype(F32)
    rows = bond_out.T.astype(BF16)
    for slot in range(slots):
        bond_result_ref[0, 0, :, slot * feature : (slot + 1) * feature] = rows[
            slot * atoms : (slot + 1) * atoms
        ]
    pooled = bond_out[:, 0:128]
    for block in range(1, blocks):
        pooled = pooled + bond_out[:, block * 128 : (block + 1) * 128]
    shift = 64
    while shift >= atoms:
        pooled = pooled + pltpu.roll(pooled, shift, 1)
        shift //= 2
    pooled = (pooled * (1.0 / slots)).astype(BF16)
    atom = values_ref[0:feature, 0:128]
    joined = jnp.concatenate([atom, pooled], axis=0)
    atom_hidden = doubled_gate(
        jnp.dot(atom_in_weight_ref[...], joined, preferred_element_type=F32)
    ).astype(BF16)
    atom_new = atom.astype(F32) + jnp.dot(
        atom_out_weight_ref[...], atom_hidden, preferred_element_type=F32
    )
    atom_result_ref[0, 0] = atom_new.T[0:atoms].astype(BF16)


def per_device(
    atom_feat,
    bond_feat,
    neighbours,
    bond_dirs,
    bond_in_weight,
    bond_mix_weight,
    pair_weight,
    angle_weight,
    pair_hidden_weight,
    pair_out_weight,
    atom_in_weight,
    atom_out_weight,
):
    atoms, feature = atom_feat.shape[2], atom_feat.shape[3]
    slots = neighbours.shape[3]
    bonds = atoms * slots
    degrees = angle_weight.shape[0]
    extents = (lax.axis_size("gx"), lax.axis_size("gy"))
    targets = neighbours[0, 0].T
    dirs = bond_dirs[:, 0, 0].reshape(2, atoms, slots).transpose(0, 2, 1).reshape(2, bonds)
    hbm = pl.BlockSpec(memory_space=pltpu.HBM)
    vmem = pl.BlockSpec(memory_space=pltpu.VMEM)
    params = pltpu.CompilerParams(vmem_limit_bytes=32 * 2**20)

    def shaped(shape, dtype):
        return jax.ShapeDtypeStruct(shape, dtype)

    payload = shaped((3 * CAP, 2 * feature), BF16)
    own, one, two = pl.pallas_call(
        functools.partial(pack_kernel, extents),
        out_shape=(payload, payload, payload),
        in_specs=[hbm, hbm, hbm],
        out_specs=(vmem, vmem, vmem),
        scratch_shapes=[
            pltpu.VMEM(targets.shape, jnp.int32),
            pltpu.VMEM(atom_feat.shape, BF16),
            pltpu.VMEM(bond_feat.shape, BF16),
            pltpu.SemaphoreType.DMA((3,)),
        ],
        compiler_params=params,
        name="pack",
    )(*(pltpu.with_memory_space_constraint(x, pltpu.HBM) for x in (targets, atom_feat, bond_feat)))
    first, second = partners(extents[0])
    one = lax.ppermute(one, "gx", first)
    two = lax.ppermute(two, "gx", second)
    basis = pl.pallas_call(
        functools.partial(basis_kernel, atoms),
        out_shape=shaped((slots, degrees, bonds), BF16),
        in_specs=[vmem],
        out_specs=vmem,
        compiler_params=params,
        cost_estimate=pl.CostEstimate(flops=4 * 2**20, bytes_accessed=2**20, transcendentals=4096),
        name="basis",
    )(dirs)
    own, one, two, basis = lax.optimization_barrier((own, one, two, basis))
    first, second = partners(extents[1])
    near = jnp.concatenate([x[CAP : 2 * CAP] for x in (own, one, two)], axis=0)
    away = jnp.concatenate([x[2 * CAP :] for x in (own, one, two)], axis=0)
    three = lax.ppermute(near, "gy", first)
    four = lax.ppermute(away, "gy", second)
    weights = (
        shaped((4 * feature, 2 * feature), BF16),
        shaped((2 * feature, 2 * feature), BF16),
        shaped((4 * feature, feature), BF16),
        shaped((2 * feature, degrees), BF16),
        shaped((2 * feature, feature), BF16),
        shaped((feature, feature), BF16),
        shaped((2 * feature, 2 * feature), BF16),
        shaped((feature, feature), BF16),
    )
    prepared = pl.pallas_call(
        functools.partial(prepare_kernel, extents),
        out_shape=(
            shaped((9 * CAP, bonds), BF16),
            shaped((2 * feature, bonds), BF16),
            shaped((4 * feature, bonds), F32),
        )
        + weights,
        in_specs=[vmem] * 11,
        out_specs=(vmem,) * 11,
        compiler_params=params,
        cost_estimate=pl.CostEstimate(flops=64 * 2**20, bytes_accessed=2**21, transcendentals=0),
        name="prepare",
    )(
        targets,
        atom_feat,
        bond_feat,
        bond_in_weight,
        bond_mix_weight,
        pair_weight,
        angle_weight,
        pair_hidden_weight,
        pair_out_weight,
        atom_in_weight,
        atom_out_weight,
    )
    return pl.pallas_call(
        main_kernel,
        out_shape=(shaped(atom_feat.shape, BF16), shaped(bond_feat.shape, BF16)),
        in_specs=[vmem] * 17,
        out_specs=(vmem, vmem),
        scratch_shapes=[
            pltpu.VMEM((2 * feature, bonds), F32),
            pltpu.VMEM((128 // atoms, 2 * feature, bonds), F32),
        ],
        compiler_params=params,
        cost_estimate=pl.CostEstimate(
            flops=400 * 2**20, bytes_accessed=2**22, transcendentals=2**21
        ),
        name="main",
    )(own, one, two, three, four, basis, *prepared)


def solution(mesh):
    placed = (
        P("gx", "gy", None, None),
        P("gx", "gy", None, None),
        P("gx", "gy", None, None),
        P(None, "gx", "gy", None),
        P(),
        P(),
        P(),
        P(),
        P(),
        P(),
        P(),
        P(),
    )
    return jax.shard_map(
        per_device,
        mesh=mesh,
        in_specs=placed,
        out_specs=(P("gx", "gy", None, None), P("gx", "gy", None, None)),
        check_vma=False,
    )
```

profile of v0, /device:TPU:0, one launch (start us, length us, event | category | flops | bytes accessed | tf_op | source)
XLA Modules:
  0.0 19.2 jit_solution(637867660952346698)
XLA Ops:
  0.6 0.0 copy-start.11
  0.6 1.4 %pack.1 = (bf16[192,128]{1,0:T(8,128)(2,1)S(1)}, bf16[192,128]{1,0:T(8,128)(2,1)S(1)}, bf16[192,128]{1,0:T(8,128)(2,1)S(1)}) custom-call(s32[16,32]{1,0:T(8,128)} %bitcast.4, bf16[1,1,32,64]{3,2,1,0:T(8,128)(2,1)} %atom_ref.1, bf16[1,1,32,1024]{3,2,1,0:T(8,128)(2,1)} %bond_ref.1), custom_call_target="tpu_custom_call" | custom-call | tf_op jit(solution)/shard_map/pack/pallas_call | solution.py:378
  2.0 0.5 %collective-permute-start = (bf16[192,128]{1,0:T(8,128)(2,1)S(1)}, bf16[192,128]{1,0:T(8,128)(2,1)S(1)}, u32[]{:S(2)}, u32[]{:S(2)}) collective-permute-start(bf16[192,128]{1,0:T(8,128)(2,1)S(1)} %get-tuple-element.21), channel_id=1, source_target_pairs={{0,8},{8,0},{16,24},{24,16},{1,9},{9,1},{17,25},{25,17},{2,10},{10... | collective-permute-start | bytes 147464 | tf_op jit(solution)/shard_map/ppermute | solution.py:393
  2.5 2.6 %collective-permute-start.1 = (bf16[192,128]{1,0:T(8,128)(2,1)S(1)}, bf16[192,128]{1,0:T(8,128)(2,1)S(1)}, u32[]{:S(2)}, u32[]{:S(2)}) collective-permute-start(bf16[192,128]{1,0:T(8,128)(2,1)S(1)} %get-tuple-element.22), channel_id=1, source_target_pairs={{0,24},{8,16},{16,8},{24,0},{1,25},{9,17},{17,9},{25,1},{2,26},{10... | collective-permute-start | bytes 147464 | tf_op jit(solution)/shard_map/ppermute | solution.py:394
  5.1 0.0 copy-done.11
  5.2 0.1 reshape_squeeze.3
  5.2 0.1 copy.15
  5.3 0.1 reshape.7.dirs_ref
  5.4 0.5 %basis.1.basis_ref = bf16[16,64,512]{2,1,0:T(8,128)(2,1)S(1)} custom-call(f32[2,512]{1,0:T(2,128)S(1)} %reshape.7.dirs_ref), custom_call_target="tpu_custom_call" | custom-call | flops 4194304 | bytes 1048576 | tf_op jit(solution)/shard_map/basis/pallas_call | solution.py:395
  5.9 0.0 collective-permute-done.one_ref
  5.9 1.2 %collective-permute-done.1.two_ref = bf16[192,128]{1,0:T(8,128)(2,1)S(1)} collective-permute-done((bf16[192,128]{1,0:T(8,128)(2,1)S(1)}, bf16[192,128]{1,0:T(8,128)(2,1)S(1)}, u32[]{:S(2)}, u32[]{:S(2)}) %collective-permute-start.1) | collective-permute-done | bytes 49184 | tf_op jit(solution)/shard_map/ppermute | solution.py:394
  7.2 0.0 copy-start.6
  7.2 0.0 copy-start.7
  7.2 0.0 copy-start.8
  7.2 0.0 copy-start.9
  7.2 0.0 copy-start.10
  7.2 0.0 copy-start.1
  7.2 0.0 copy-start.3
  7.2 0.0 copy-start.4
  7.3 0.0 copy-start.5
  7.3 0.0 copy-start
  7.3 1.5 %collective-permute-start.2 = (bf16[192,128]{1,0:T(8,128)(2,1)S(1)}, bf16[192,128]{1,0:T(8,128)(2,1)S(1)}, u32[]{:S(2)}, u32[]{:S(2)}) collective-permute-start(bf16[192,128]{1,0:T(8,128)(2,1)S(1)} %pad_maximum_fusion), channel_id=1, source_target_pairs={{0,1},{1,0},{2,3},{3,2},{4,5},{5,4},{6,7},{7,6},{8,9},{9,8},{10,11... | collective-permute-start | bytes 147464 | tf_op jit(solution)/shard_map/ppermute | solution.py:408
  8.8 0.0 copy-start.2
  8.8 3.5 %collective-permute-start.3 = (bf16[192,128]{1,0:T(8,128)(2,1)S(1)}, bf16[192,128]{1,0:T(8,128)(2,1)S(1)}, u32[]{:S(2)}, u32[]{:S(2)}) collective-permute-start(bf16[192,128]{1,0:T(8,128)(2,1)S(1)} %pad_maximum_fusion.1), channel_id=1, source_target_pairs={{0,7},{1,2},{2,1},{3,4},{4,3},{5,6},{6,5},{7,0},{8,15},{9,10},{10,... | collective-permute-start | bytes 147464 | tf_op jit(solution)/shard_map/ppermute | solution.py:409
  12.4 0.0 copy-done.6
  12.4 0.0 copy-done.7
  12.4 0.0 copy-done.8
  12.4 0.0 copy-done.9
  12.4 0.0 copy-done.10
  12.4 0.0 copy-done.1
  12.4 0.0 copy-done.3
  12.4 0.0 copy-done.4
  12.4 0.0 copy-done.5
  12.4 0.0 copy-done
  12.5 0.0 copy-done.2
  12.5 0.9 %prepare.1 = (bf16[576,512]{1,0:T(8,128)(2,1)S(1)}, bf16[128,512]{1,0:T(8,128)(2,1)S(1)}, f32[256,512]{1,0:T(8,128)S(1)}, bf16[256,128]{1,0:T(8,128)(2,1)S(1)}, ...) custom-call(s32[16,32]{1,0:T(8,128)S(1)} %bitcast.5, ...), custom_call_target="tpu_custom_call" | custom-call | flops 67108864 | bytes 2097152 | tf_op jit(solution)/shard_map/prepare/pallas_call | solution.py:420
  13.4 0.0 collective-permute-done.2.three_ref
  13.4 2.2 %collective-permute-done.3.four_ref = bf16[192,128]{1,0:T(8,128)(2,1)S(1)} collective-permute-done((bf16[192,128]{1,0:T(8,128)(2,1)S(1)}, bf16[192,128]{1,0:T(8,128)(2,1)S(1)}, u32[]{:S(2)}, u32[]{:S(2)}) %collective-permute-start.3) | collective-permute-done | bytes 49184 | tf_op jit(solution)/shard_map/ppermute | solution.py:409
  15.6 3.6 %main.1 = (bf16[1,1,32,64]{3,2,1,0:T(8,128)(2,1)}, bf16[1,1,32,1024]{3,2,1,0:T(8,128)(2,1)}) custom-call(bf16[192,128]{1,0:T(8,128)(2,1)S(1)} %get-tuple-element.23.own_ref, bf16[192,128]{1,0:T(8,128)(2,1)S(1)} %collective-permute-done.one_ref, bf16[192,128]{1,0:T(8,128)(2,1)S(1)} %collective-permute-done.1.two_ref, ...), custom_call_target="tpu_custom_call" | custom-call | flops 419430400 | bytes 4194304 | tf_op jit(solution)/shard_map/main/pallas_call | solution.py:446
  (5 shorter events, 0.0 us)
Async XLA Ops:
  0.6 4.5 %copy-start.11 = (f32[2,1,1,512]{3,2,1,0:T(1,128)S(1)}, f32[2,1,1,512]{3,2,1,0:T(1,128)}, u32[]{:S(2)}) copy-start(f32[2,1,1,512]{3,2,1,0:T(1,128)} %param.15) | copy-start | bytes 12292
  2.0 3.9 %collective-permute-start = (bf16[192,128]{1,0:T(8,128)(2,1)S(1)}, bf16[192,128]{1,0:T(8,128)(2,1)S(1)}, u32[]{:S(2)}, u32[]{:S(2)}) collective-permute-start(bf16[192,128]{1,0:T(8,128)(2,1)S(1)} %get-tuple-element.21), channel_id=1, source_target_pairs={{0,8},{8,0},{16,24},{24,16},{1,9},{9,1},{17,25},{25,17},{2,10},{10... | collective-permute-start | bytes 147464 | tf_op jit(solution)/shard_map/ppermute | solution.py:393
  2.5 4.6 %collective-permute-start.1 = (bf16[192,128]{1,0:T(8,128)(2,1)S(1)}, bf16[192,128]{1,0:T(8,128)(2,1)S(1)}, u32[]{:S(2)}, u32[]{:S(2)}) collective-permute-start(bf16[192,128]{1,0:T(8,128)(2,1)S(1)} %get-tuple-element.22), channel_id=1, source_target_pairs={{0,24},{8,16},{16,8},{24,0},{1,25},{9,17},{17,9},{25,1},{2,26},{10... | collective-permute-start | bytes 147464 | tf_op jit(solution)/shard_map/ppermute | solution.py:394
  7.2 5.2 %copy-start.6 = (bf16[64,64]{1,0:T(8,128)(2,1)S(1)}, bf16[64,64]{1,0:T(8,128)(2,1)}, u32[]{:S(2)}) copy-start(bf16[64,64]{1,0:T(8,128)(2,1)} %bond_mix_ref.1) | copy-start | bytes 24580
  7.2 5.2 %copy-start.7 = (bf16[64,128]{1,0:T(8,128)(2,1)S(1)}, bf16[64,128]{1,0:T(8,128)(2,1)}, u32[]{:S(2)}) copy-start(bf16[64,128]{1,0:T(8,128)(2,1)} %angle_ref.1) | copy-start | bytes 49156
  7.2 5.2 %copy-start.8 = (bf16[64,128]{1,0:T(8,128)(2,1)S(1)}, bf16[64,128]{1,0:T(8,128)(2,1)}, u32[]{:S(2)}) copy-start(bf16[64,128]{1,0:T(8,128)(2,1)} %pair_hidden_ref.1) | copy-start | bytes 49156
  7.2 5.2 %copy-start.9 = (bf16[64,64]{1,0:T(8,128)(2,1)S(1)}, bf16[64,64]{1,0:T(8,128)(2,1)}, u32[]{:S(2)}) copy-start(bf16[64,64]{1,0:T(8,128)(2,1)} %pair_out_ref.1) | copy-start | bytes 24580
  7.2 5.2 %copy-start.10 = (bf16[64,64]{1,0:T(8,128)(2,1)S(1)}, bf16[64,64]{1,0:T(8,128)(2,1)}, u32[]{:S(2)}) copy-start(bf16[64,64]{1,0:T(8,128)(2,1)} %atom_out_ref.1) | copy-start | bytes 24580
  7.2 5.2 %copy-start.1 = (bf16[192,128]{1,0:T(8,128)(2,1)S(1)}, bf16[192,128]{1,0:T(8,128)(2,1)}, u32[]{:S(2)}) copy-start(bf16[192,128]{1,0:T(8,128)(2,1)} %bond_in_ref.1) | copy-start | bytes 147460
  7.2 5.2 %copy-start.3 = (bf16[128,128]{1,0:T(8,128)(2,1)S(1)}, bf16[128,128]{1,0:T(8,128)(2,1)}, u32[]{:S(2)}) copy-start(bf16[128,128]{1,0:T(8,128)(2,1)} %atom_in_ref.1) | copy-start | bytes 98308
  7.2 5.2 %copy-start.4 = (s32[1,1,32,16]{2,3,1,0:T(8,128)S(1)}, s32[1,1,32,16]{2,3,1,0:T(8,128)}, u32[]{:S(2)}) copy-start(s32[1,1,32,16]{2,3,1,0:T(8,128)} %param.14) | copy-start | bytes 6148
  7.3 5.2 %copy-start.5 = (bf16[1,1,32,64]{3,2,1,0:T(8,128)(2,1)S(1)}, bf16[1,1,32,64]{3,2,1,0:T(8,128)(2,1)}, u32[]{:S(2)}) copy-start(bf16[1,1,32,64]{3,2,1,0:T(8,128)(2,1)} %atom_ref.1) | copy-start | bytes 12292
  7.3 5.2 %copy-start = (bf16[1,1,32,1024]{3,2,1,0:T(8,128)(2,1)S(1)}, bf16[1,1,32,1024]{3,2,1,0:T(8,128)(2,1)}, u32[]{:S(2)}) copy-start(bf16[1,1,32,1024]{3,2,1,0:T(8,128)(2,1)} %bond_ref.1) | copy-start | bytes 196612
  7.3 6.1 %collective-permute-start.2 = (bf16[192,128]{1,0:T(8,128)(2,1)S(1)}, bf16[192,128]{1,0:T(8,128)(2,1)S(1)}, u32[]{:S(2)}, u32[]{:S(2)}) collective-permute-start(bf16[192,128]{1,0:T(8,128)(2,1)S(1)} %pad_maximum_fusion), channel_id=1, source_target_pairs={{0,1},{1,0},{2,3},{3,2},{4,5},{5,4},{6,7},{7,6},{8,9},{9,8},{10,11... | collective-permute-start | bytes 147464 | tf_op jit(solution)/shard_map/ppermute | solution.py:408
  8.8 3.6 %copy-start.2 = (bf16[64,256]{1,0:T(8,128)(2,1)S(1)}, bf16[64,256]{1,0:T(8,128)(2,1)}, u32[]{:S(2)}) copy-start(bf16[64,256]{1,0:T(8,128)(2,1)} %pair_ref.1) | copy-start | bytes 98308
  8.8 6.8 %collective-permute-start.3 = (bf16[192,128]{1,0:T(8,128)(2,1)S(1)}, bf16[192,128]{1,0:T(8,128)(2,1)S(1)}, u32[]{:S(2)}, u32[]{:S(2)}) collective-permute-start(bf16[192,128]{1,0:T(8,128)(2,1)S(1)} %pad_maximum_fusion.1), channel_id=1, source_target_pairs={{0,7},{1,2},{2,1},{3,4},{4,3},{5,6},{6,5},{7,0},{8,15},{9,10},{10,... | collective-permute-start | bytes 147464 | tf_op jit(solution)/shard_map/ppermute | solution.py:409
where the time goes:
time: 19.4 us; the launch traced here: 19.2 us
  starting transfers between devices  8.22 us (42%)
  Pallas kernels  6.37 us (33%)
  waiting for transfers between devices  3.49 us (18%)
  between operations  0.82 us (4%)
  local copies, waits for them, and re-layouts  0.32 us (2%)
    pallas_call x1, Pallas kernels, per_device(): pl.pallas_call(main_kernel, out_shape=(shaped(atom_feat.shape, BF16), sha...  3.62 us
    ppermute x1, starting transfers between devices, per_device(): four = lax.ppermute(away, 'gy', second)  3.55 us
    ppermute x1, starting transfers between devices, per_device(): two = lax.ppermute(two, 'gx', second)  2.61 us
    ppermute x1, waiting for transfers between devices, per_device(): four = lax.ppermute(away, 'gy', second)  2.24 us
    ppermute x1, starting transfers between devices, per_device(): three = lax.ppermute(near, 'gy', first)  1.54 us
    pallas_call x1, Pallas kernels, per_device(): pl.pallas_call(functools.partial(pack_kernel, extents), out_shape=(payloa...  1.35 us
    ppermute x1, waiting for transfers between devices, per_device(): two = lax.ppermute(two, 'gx', second)  1.24 us
    pallas_call x1, Pallas kernels, per_device(): pl.pallas_call(functools.partial(prepare_kernel, extents), out_shape=(sha...  0.9 us
  transfers between devices with their start and end apart: 4, of which 2 were waited for; matrix products, arithmetic and copies ran while one was open for 1% of the time, Pallas kernels for 7%

commit v1 on v0

--- a/solution.py
+++ b/solution.py
@@ -24,36 +24,27 @@
     return lax.rem(values, jnp.int32(size))
 
 
-def step_code(owner, home, extent, receives):
+def step_code(owner, home, extent, paired, receives):
     step = remainder(owner - home + 1 + extent, extent)
-    if extent % 2 == 0:
-        first = remainder(home, 2) == 0
-        ahead = jnp.where(first, 2, 0)
+    if paired:
+        ahead = jnp.where(remainder(home, 2) == 0, 0, 2)
     else:
         ahead = 0 if receives else 2
     return jnp.where(step == 1, 0, jnp.where(step == ahead, 1, 2))
 
 
-def partners(extent):
-    if extent % 2 == 0:
-        one = [(i, i ^ 1) for i in range(extent)]
-        two = [(i, ((i + 1) ^ 1) - 1) for i in range(extent)]
-        two = [(i, j % extent) for i, j in two]
-        return one, two
-    return (
-        [(i, (i + 1) % extent) for i in range(extent)],
-        [((i + 1) % extent, i) for i in range(extent)],
-    )
-
-
-def own_rows(atom_ref, bond_ref, slots):
-    atom = atom_ref[0, 0].astype(F32)
-    feature = atom.shape[1]
-    rows = []
-    for slot in range(slots):
-        bond = bond_ref[0, 0, :, slot * feature : (slot + 1) * feature].astype(F32)
-        rows.append(jnp.concatenate([atom, bond], axis=1))
-    return jnp.concatenate(rows, axis=0).astype(BF16)
+def moves(extent, paired):
+    if paired:
+        near = [(i, i ^ 1) for i in range(extent)]
+        return [(i, (((i + 1) ^ 1) - 1) % extent) for i in range(extent)], near
+    up = [(i, (i + 1) % extent) for i in range(extent)]
+    return up, [(j, i) for i, j in up]
+
+
+def bond_rows(bond_ref, slots):
+    feature = bond_ref.shape[3] // slots
+    rows = [bond_ref[0, 0, :, slot * feature : (slot + 1) * feature] for slot in range(slots)]
+    return jnp.concatenate(rows, axis=0)
 
 
 def slot_major(table):
@@ -69,15 +60,18 @@
     return jnp.concatenate(pieces, axis=1).astype(jnp.int32)
 
 
-def bond_codes(targets, atoms, extents, receives):
+def bond_codes(targets, atoms, extents, paired, receives):
     owner = quotient(targets, atoms)
-    code_x = step_code(quotient(owner, extents[1]), lax.axis_index("gx"), extents[0], receives)
-    code_y = step_code(remainder(owner, extents[1]), lax.axis_index("gy"), extents[1], receives)
-    return code_x, code_y
+    block = (quotient(owner, extents[1]), remainder(owner, extents[1]))
+    return tuple(
+        step_code(block[k], lax.axis_index(axis), extents[k], paired[k], receives)
+        for k, axis in enumerate(("gx", "gy"))
+    )
 
 
 def pack_kernel(
     extents,
+    paired,
     targets_hbm,
     atom_hbm,
     bond_hbm,
@@ -103,7 +97,9 @@
     lanes = 128
     groups = bonds // lanes
     copies[0].wait()
-    code_x, code_y = bond_codes(slot_major(targets_ref[...]), atoms, extents, False)
+    code_x, code_y = bond_codes(
+        slot_major(targets_ref[...]), atoms, extents, paired, False
+    )
     code = 3 * code_x + code_y
     rows = lax.broadcasted_iota(jnp.int32, (16, lanes), 0)
     marks = [rows == code[:, g * lanes : (g + 1) * lanes] for g in range(groups)]
@@ -120,14 +116,24 @@
             jnp.sum(jnp.where(marks[g], part[:, :lanes] + earlier, 0.0), axis=0, keepdims=True)
         )
         earlier = earlier + part[:, lanes:]
-    place = jnp.concatenate(place, axis=1).astype(jnp.int32) + CAP * code
+    place = jnp.concatenate(place, axis=1).astype(jnp.int32)
+    row_count = 3 * CAP // 2
+    spot = lax.broadcasted_iota(jnp.int32, (row_count, bonds), 0)
     copies[1].wait()
     copies[2].wait()
-    values = own_rows(atom_ref, bond_ref, slots)
+    values = bond_rows(bond_ref, slots)
+    atom = atom_ref[0, 0]
+    atom = jnp.concatenate([atom[: atoms // 2], atom[atoms // 2 :]], axis=1)
     for third, ref in enumerate((own_ref, one_ref, two_ref)):
-        spot = lax.broadcasted_iota(jnp.int32, (3 * CAP, bonds), 0) + 3 * CAP * third
-        chosen = jnp.where(spot == place, 1.0, 0.0).astype(BF16)
-        ref[...] = jnp.dot(chosen, values, preferred_element_type=F32).astype(BF16)
+        halves = []
+        for half in range(2):
+            inside = quotient(place, CAP // 2) == half
+            wanted = place - half * (CAP // 2) + (code - 3 * third) * (CAP // 2)
+            wanted = jnp.where(inside, wanted, -1)
+            chosen = jnp.where(spot == wanted, 1.0, 0.0).astype(BF16)
+            halves.append(jnp.dot(chosen, values, preferred_element_type=F32))
+        ref[:row_count] = jnp.concatenate(halves, axis=1).astype(BF16)
+        ref[row_count:] = atom
 
 
 def basis_kernel(atoms, dirs_ref, basis_ref):
@@ -167,6 +173,7 @@
 
 def prepare_kernel(
     extents,
+    paired,
     targets_ref,
     atom_ref,
     bond_ref,
@@ -178,7 +185,9 @@
     pair_out_ref,
     atom_in_ref,
     atom_out_ref,
-    chosen_ref,
+    chosen_bond_ref,
+    chosen_atom_ref,
+    right_half_ref,
     values_ref,
     near_ref,
     far_weight_ref,
@@ -195,7 +204,7 @@
     slots = targets_ref.shape[0]
     bonds = slots * atoms
     targets = slot_major(targets_ref[...])
-    code_x, code_y = bond_codes(targets, atoms, extents, True)
+    code_x, code_y = bond_codes(targets, atoms, extents, paired, True)
     code = 3 * code_y + code_x
     bond = lax.broadcasted_iota(jnp.int32, (1, bonds), 1)
     far = (slots - 1 - quotient(bond, atoms)) * atoms + remainder(targets, atoms)
@@ -207,11 +216,23 @@
         here = slice(group * 128, (group + 1) * 128)
         inside = (column < key[:, here]) & (column >= base[:, here])
         place.append(jnp.sum(jnp.where(inside, 1.0, 0.0), axis=0, keepdims=True))
-    place = jnp.concatenate(place, axis=1).astype(jnp.int32) + CAP * code
-    spot = lax.broadcasted_iota(jnp.int32, (9 * CAP, bonds), 0)
-    chosen_ref[...] = jnp.where(spot == place, 1.0, 0.0).astype(BF16)
-
-    values = own_rows(atom_ref, bond_ref, slots).astype(F32).T.astype(BF16)
+    place = jnp.concatenate(place, axis=1).astype(jnp.int32)
+    half = CAP // 2
+    spot = lax.broadcasted_iota(jnp.int32, (9 * half, bonds), 0)
+    wanted = remainder(place, half) + half * code
+    chosen_bond_ref[...] = jnp.where(spot == wanted, 1.0, 0.0).astype(BF16)
+    spot = lax.broadcasted_iota(jnp.int32, (9 * atoms // 2, bonds), 0)
+    atom = remainder(targets, atoms)
+    wanted = remainder(atom, atoms // 2) + atoms // 2 * code
+    chosen_atom_ref[...] = jnp.where(spot == wanted, 1.0, 0.0).astype(BF16)
+    row = lax.broadcasted_iota(jnp.int32, (8, bonds), 0)
+    right_half = jnp.where(row == 0, quotient(place, half), quotient(atom, atoms // 2))
+    right_half_ref[...] = right_half.astype(F32)
+
+    atom = atom_ref[0, 0].astype(F32)
+    atom = jnp.concatenate([atom] * slots, axis=0)
+    values = jnp.concatenate([atom, bond_rows(bond_ref, slots).astype(F32)], axis=1)
+    values = values.T.astype(BF16)
     values_ref[...] = values
 
     def turned(weight, scale):
@@ -253,10 +274,12 @@
     own_ref,
     one_ref,
     two_ref,
+    four_ref,
     three_ref,
-    four_ref,
     basis_ref,
-    chosen_ref,
+    chosen_bond_ref,
+    chosen_atom_ref,
+    right_half_ref,
     values_ref,
     near_ref,
     far_weight_ref,
@@ -275,18 +298,33 @@
     slots, degrees, bonds = basis_ref.shape
     atoms = bonds // slots
     feature = values_ref.shape[0] // 2
-    received = jnp.concatenate(
-        [own_ref[0:CAP], one_ref[0:CAP], two_ref[0:CAP], three_ref[...], four_ref[...]], axis=0
-    )
-    received = received.astype(F32).T.astype(BF16)
-    far = jnp.dot(received, chosen_ref[...], preferred_element_type=F32)
+    half = CAP // 2
+    near_refs = (own_ref, one_ref, two_ref)
+    away_refs = (three_ref, four_ref)
+
+    def unpacked(parts, chosen, right_half):
+        rows = jnp.concatenate(parts, axis=0).astype(F32).T.astype(BF16)
+        both = jnp.dot(rows, chosen, preferred_element_type=F32)
+        return jnp.where(right_half > 0.0, both[feature:], both[:feature])
+
+    far_bond = unpacked(
+        [ref[:half] for ref in near_refs] + [ref[: 3 * half] for ref in away_refs],
+        chosen_bond_ref[...],
+        right_half_ref[0:1],
+    )
+    far_atom = unpacked(
+        [ref[3 * half :] for ref in near_refs + away_refs],
+        chosen_atom_ref[...],
+        right_half_ref[1:2],
+    )
+    far = jnp.concatenate([far_atom, far_bond], axis=0)
     incoming = near_ref[...] + jnp.dot(
         far_weight_ref[...], far.astype(BF16), preferred_element_type=F32
     )
     hidden = doubled_gate(incoming).astype(BF16)
     mixed = jnp.dot(mix_weight_ref[...], hidden, preferred_element_type=F32)
     ahead = (values_ref[feature:].astype(F32) + mixed[:feature]).astype(BF16).astype(F32)
-    back = (far[feature:] + mixed[feature:]).astype(BF16).astype(F32)
+    back = (far_bond + mixed[feature:]).astype(BF16).astype(F32)
     average = ((ahead + back) * 0.5).astype(BF16)
     projected = jnp.dot(pair_weight_ref[...], average, preferred_element_type=F32)
     first_ref[...] = projected[: 2 * feature]
@@ -374,9 +412,11 @@
     def shaped(shape, dtype):
         return jax.ShapeDtypeStruct(shape, dtype)
 
-    payload = shaped((3 * CAP, 2 * feature), BF16)
+    paired = (extents[0] % 2 == 0, False)
+    half = CAP // 2
+    payload = shaped((3 * half + atoms // 2, 2 * feature), BF16)
     own, one, two = pl.pallas_call(
-        functools.partial(pack_kernel, extents),
+        functools.partial(pack_kernel, extents, paired),
         out_shape=(payload, payload, payload),
         in_specs=[hbm, hbm, hbm],
         out_specs=(vmem, vmem, vmem),
@@ -389,7 +429,7 @@
         compiler_params=params,
         name="pack",
     )(*(pltpu.with_memory_space_constraint(x, pltpu.HBM) for x in (targets, atom_feat, bond_feat)))
-    first, second = partners(extents[0])
+    first, second = moves(extents[0], paired[0])
     one = lax.ppermute(one, "gx", first)
     two = lax.ppermute(two, "gx", second)
     basis = pl.pallas_call(
@@ -402,11 +442,14 @@
         name="basis",
     )(dirs)
     own, one, two, basis = lax.optimization_barrier((own, one, two, basis))
-    first, second = partners(extents[1])
-    near = jnp.concatenate([x[CAP : 2 * CAP] for x in (own, one, two)], axis=0)
-    away = jnp.concatenate([x[2 * CAP :] for x in (own, one, two)], axis=0)
-    three = lax.ppermute(near, "gy", first)
-    four = lax.ppermute(away, "gy", second)
+    first, second = moves(extents[1], paired[1])
+
+    def forwarded(block):
+        parts = [x[block * half : (block + 1) * half] for x in (own, one, two)]
+        return jnp.concatenate(parts + [x[3 * half :] for x in (own, one, two)], axis=0)
+
+    three = lax.ppermute(forwarded(1), "gy", first)
+    four = lax.ppermute(forwarded(2), "gy", second)
     weights = (
         shaped((4 * feature, 2 * feature), BF16),
         shaped((2 * feature, 2 * feature), BF16),
@@ -418,15 +461,17 @@
         shaped((feature, feature), BF16),
     )
     prepared = pl.pallas_call(
-        functools.partial(prepare_kernel, extents),
+        functools.partial(prepare_kernel, extents, paired),
         out_shape=(
-            shaped((9 * CAP, bonds), BF16),
+            shaped((9 * half, bonds), BF16),
+            shaped((9 * atoms // 2, bonds), BF16),
+            shaped((8, bonds), F32),
             shaped((2 * feature, bonds), BF16),
             shaped((4 * feature, bonds), F32),
         )
         + weights,
         in_specs=[vmem] * 11,
-        out_specs=(vmem,) * 11,
+        out_specs=(vmem,) * 13,
         compiler_params=params,
         cost_estimate=pl.CostEstimate(flops=64 * 2**20, bytes_accessed=2**21, transcendentals=0),
         name="prepare",
@@ -446,7 +491,7 @@
     return pl.pallas_call(
         main_kernel,
         out_shape=(shaped(atom_feat.shape, BF16), shaped(bond_feat.shape, BF16)),
-        in_specs=[vmem] * 17,
+        in_specs=[vmem] * 19,
         out_specs=(vmem, vmem),
         scratch_shapes=[
             pltpu.VMEM((2 * feature, bonds), F32),
@@ -457,7 +502,7 @@
             flops=400 * 2**20, bytes_accessed=2**22, transcendentals=2**21
         ),
         name="main",
-    )(own, one, two, three, four, basis, *prepared)
+    )(own, one, two, four, three, basis, *prepared)
 
 
 def solution(mesh):

time: 19.4 us -> 17.6 us (0.907)
  waiting for transfers between devices: 3.49 us -> 1.12 us
  starting transfers between devices: 8.22 us -> 8.74 us
    ppermute x1, starting transfers between devices: 2.61 us -> 0.67 us  [per_device(): two = lax.ppermute(two, 'gx', second)]
    ppermute x1, starting transfers between devices: 0.52 us -> 2.44 us  [per_device(): one = lax.ppermute(one, 'gx', first)]
    ppermute x2, waiting for transfers between devices: 2.24 us -> 0.93 us  [the longest x1 0.93 us: per_device(): three = lax.ppermute(forwarded(1), 'gy', first)]
    ppermute x1, waiting for transfers between devices: 1.24 us -> 0.01 us  [per_device(): two = lax.ppermute(two, 'gx', second)]
    ppermute x2, starting transfers between devices: 5.08 us -> 5.62 us  [the longest x1 3.12 us: per_device(): four = lax.ppermute(forwarded(2), 'gy', second)]
  transfers between devices with their start and end apart: 4 -> 4, of which waited for: 2 -> 2; matrix products, arithmetic and copies ran while one was open for 1% -> 1% of each run, Pallas kernels for 7% -> 8%
where the time goes in v1:
time: 17.6 us; the launch traced here: 17.4 us
  starting transfers between devices  8.74 us (50%)
  Pallas kernels  6.4 us (36%)
  waiting for transfers between devices  1.12 us (6%)
  between operations  0.81 us (5%)
  local copies, waits for them, and re-layouts  0.35 us (2%)
    pallas_call x1, Pallas kernels, per_device(): pl.pallas_call(main_kernel, out_shape=(shaped(atom_feat.shape, BF16), sha...  3.63 us
    ppermute x1, starting transfers between devices, per_device(): four = lax.ppermute(forwarded(2), 'gy', second)  3.12 us
    ppermute x1, starting transfers between devices, per_device(): three = lax.ppermute(forwarded(1), 'gy', first)  2.5 us
    ppermute x1, starting transfers between devices, per_device(): one = lax.ppermute(one, 'gx', first)  2.44 us
    pallas_call x1, Pallas kernels, per_device(): pl.pallas_call(functools.partial(pack_kernel, extents, paired), out_shape...  1.42 us
    ppermute x1, waiting for transfers between devices, per_device(): three = lax.ppermute(forwarded(1), 'gy', first)  0.93 us
    pallas_call x1, Pallas kernels, per_device(): pl.pallas_call(functools.partial(prepare_kernel, extents, paired), out_sh...  0.85 us
    ppermute x1, starting transfers between devices, per_device(): two = lax.ppermute(two, 'gx', second)  0.67 us
  transfers between devices with their start and end apart: 4, of which 2 were waited for; matrix products, arithmetic and copies ran while one was open for 1% of the time, Pallas kernels for 8%

profile of v1, /device:TPU:0, one launch (start us, length us, event | category | flops | bytes accessed | tf_op | source)
XLA Modules:
  0.0 17.4 jit_solution(18345869404229539612)
XLA Ops:
  0.6 0.0 copy-start.11
  0.6 1.4 %pack.1 = (bf16[112,128]{1,0:T(8,128)(2,1)S(1)}, bf16[112,128]{1,0:T(8,128)(2,1)S(1)}, bf16[112,128]{1,0:T(8,128)(2,1)S(1)}) custom-call(s32[16,32]{1,0:T(8,128)} %bitcast.4, bf16[1,1,32,64]{3,2,1,0:T(8,128)(2,1)} %atom_ref.1, bf16[1,1,32,1024]{3,2,1,0:T(8,128)(2,1)} %bond_ref.1), custom_call_target="tpu_custom_call" | custom-call | tf_op jit(solution)/shard_map/pack/pallas_call | solution.py:418
  2.1 2.4 %collective-permute-start = (bf16[112,128]{1,0:T(8,128)(2,1)S(1)}, bf16[112,128]{1,0:T(8,128)(2,1)S(1)}, u32[]{:S(2)}, u32[]{:S(2)}) collective-permute-start(bf16[112,128]{1,0:T(8,128)(2,1)S(1)} %get-tuple-element.23), channel_id=1, source_target_pairs={{0,24},{8,16},{16,8},{24,0},{1,25},{9,17},{17,9},{25,1},{2,26},{10... | collective-permute-start | bytes 86024 | tf_op jit(solution)/shard_map/ppermute | solution.py:433
  4.5 0.7 %collective-permute-start.1 = (bf16[112,128]{1,0:T(8,128)(2,1)S(1)}, bf16[112,128]{1,0:T(8,128)(2,1)S(1)}, u32[]{:S(2)}, u32[]{:S(2)}) collective-permute-start(bf16[112,128]{1,0:T(8,128)(2,1)S(1)} %get-tuple-element.24), channel_id=1, source_target_pairs={{0,8},{8,0},{16,24},{24,16},{1,9},{9,1},{17,25},{25,17},{2,10},{10... | collective-permute-start | bytes 86024 | tf_op jit(solution)/shard_map/ppermute | solution.py:434
  5.2 0.0 copy-done.11
  5.2 0.1 reshape_squeeze.3
  5.3 0.1 copy.15
  5.4 0.1 reshape.7.dirs_ref
  5.4 0.0 copy-start.3
  5.4 0.0 copy-start.5
  5.5 0.0 copy-start.6
  5.5 0.0 copy-start.7
  5.5 0.0 copy-start.8
  5.5 0.0 copy-start.9
  5.5 0.0 copy-start.10
  5.5 0.5 %basis.1.basis_ref = bf16[16,64,512]{2,1,0:T(8,128)(2,1)S(1)} custom-call(f32[2,512]{1,0:T(2,128)S(1)} %reshape.7.dirs_ref), custom_call_target="tpu_custom_call" | custom-call | flops 4194304 | bytes 1048576 | tf_op jit(solution)/shard_map/basis/pallas_call | solution.py:435
  6.0 0.2 %collective-permute-done.one_ref = bf16[112,128]{1,0:T(8,128)(2,1)S(1)} collective-permute-done((bf16[112,128]{1,0:T(8,128)(2,1)S(1)}, bf16[112,128]{1,0:T(8,128)(2,1)S(1)}, u32[]{:S(2)}, u32[]{:S(2)}) %collective-permute-start) | collective-permute-done | bytes 28704 | tf_op jit(solution)/shard_map/ppermute | solution.py:433
  6.2 0.0 collective-permute-done.1.two_ref
  6.2 0.0 copy-start.2
  6.2 0.0 copy-start
  6.2 0.0 copy-start.1
  6.3 0.0 copy-start.4
  6.3 2.5 %collective-permute-start.3 = (bf16[144,128]{1,0:T(8,128)(2,1)S(1)}, bf16[144,128]{1,0:T(8,128)(2,1)S(1)}, u32[]{:S(2)}, u32[]{:S(2)}) collective-permute-start(bf16[144,128]{1,0:T(8,128)(2,1)S(1)} %get-tuple-element.42), channel_id=1, source_target_pairs={{0,1},{1,2},{2,3},{3,4},{4,5},{5,6},{6,7},{7,0},{8,9},{9,10},{10,1... | collective-permute-start | bytes 110600 | tf_op jit(solution)/shard_map/ppermute | solution.py:451
  8.8 3.1 %collective-permute-start.2 = (bf16[144,128]{1,0:T(8,128)(2,1)S(1)}, bf16[144,128]{1,0:T(8,128)(2,1)S(1)}, u32[]{:S(2)}, u32[]{:S(2)}) collective-permute-start(bf16[144,128]{1,0:T(8,128)(2,1)S(1)} %get-tuple-element.43), channel_id=1, source_target_pairs={{1,0},{2,1},{3,2},{4,3},{5,4},{6,5},{7,6},{0,7},{9,8},{10,9},{11,1... | collective-permute-start | bytes 110600 | tf_op jit(solution)/shard_map/ppermute | solution.py:452
  11.9 0.0 copy-done.3
  11.9 0.0 copy-done.5
  11.9 0.0 copy-done.6
  11.9 0.0 copy-done.7
  11.9 0.0 copy-done.8
  12.0 0.0 copy-done.9
  12.0 0.0 copy-done.10
  12.0 0.0 copy-done.2
  12.0 0.0 copy-done
  12.0 0.0 copy-done.1
  12.0 0.0 copy-done.4
  12.0 0.9 %prepare.1 = (bf16[288,512]{1,0:T(8,128)(2,1)S(1)}, bf16[144,512]{1,0:T(8,128)(2,1)S(1)}, f32[8,512]{1,0:T(8,128)S(1)}, bf16[128,512]{1,0:T(8,128)(2,1)S(1)}, f3...) custom-call(s32[16,32]{1,0:T(8,128)S(1)} %bitcast.5, ...), custom_call_target="tpu_custom_call" | custom-call | flops 67108864 | bytes 2097152 | tf_op jit(solution)/shard_map/prepare/pallas_call | solution.py:463
  12.9 0.9 %collective-permute-done.3.three_ref = bf16[144,128]{1,0:T(8,128)(2,1)S(1)} collective-permute-done((bf16[144,128]{1,0:T(8,128)(2,1)S(1)}, bf16[144,128]{1,0:T(8,128)(2,1)S(1)}, u32[]{:S(2)}, u32[]{:S(2)}) %collective-permute-start.3) | collective-permute-done | bytes 36896 | tf_op jit(solution)/shard_map/ppermute | solution.py:451
  13.8 0.0 collective-permute-done.2.four_ref
  13.8 3.6 %main.1 = (bf16[1,1,32,64]{3,2,1,0:T(8,128)(2,1)}, bf16[1,1,32,1024]{3,2,1,0:T(8,128)(2,1)}) custom-call(bf16[112,128]{1,0:T(8,128)(2,1)S(1)} %get-tuple-element.25.own_ref, bf16[112,128]{1,0:T(8,128)(2,1)S(1)} %collective-permute-done.one_ref, bf16[112,128]{1,0:T(8,128)(2,1)S(1)} %collective-permute-done.1.two_ref, ...), custom_call_target="tpu_custom_call" | custom-call | flops 419430400 | bytes 4194304 | tf_op jit(solution)/shard_map/main/pallas_call | solution.py:491
  (7 shorter events, 0.1 us)
Async XLA Ops:
  0.6 4.6 %copy-start.11 = (f32[2,1,1,512]{3,2,1,0:T(1,128)S(1)}, f32[2,1,1,512]{3,2,1,0:T(1,128)}, u32[]{:S(2)}) copy-start(f32[2,1,1,512]{3,2,1,0:T(1,128)} %param.15) | copy-start | bytes 12292
  2.1 4.1 %collective-permute-start = (bf16[112,128]{1,0:T(8,128)(2,1)S(1)}, bf16[112,128]{1,0:T(8,128)(2,1)S(1)}, u32[]{:S(2)}, u32[]{:S(2)}) collective-permute-start(bf16[112,128]{1,0:T(8,128)(2,1)S(1)} %get-tuple-element.23), channel_id=1, source_target_pairs={{0,24},{8,16},{16,8},{24,0},{1,25},{9,17},{17,9},{25,1},{2,26},{10... | collective-permute-start | bytes 86024 | tf_op jit(solution)/shard_map/ppermute | solution.py:433
  4.5 1.7 %collective-permute-start.1 = (bf16[112,128]{1,0:T(8,128)(2,1)S(1)}, bf16[112,128]{1,0:T(8,128)(2,1)S(1)}, u32[]{:S(2)}, u32[]{:S(2)}) collective-permute-start(bf16[112,128]{1,0:T(8,128)(2,1)S(1)} %get-tuple-element.24), channel_id=1, source_target_pairs={{0,8},{8,0},{16,24},{24,16},{1,9},{9,1},{17,25},{25,17},{2,10},{10... | collective-permute-start | bytes 86024 | tf_op jit(solution)/shard_map/ppermute | solution.py:434
  5.4 6.5 %copy-start.3 = (bf16[128,128]{1,0:T(8,128)(2,1)S(1)}, bf16[128,128]{1,0:T(8,128)(2,1)}, u32[]{:S(2)}) copy-start(bf16[128,128]{1,0:T(8,128)(2,1)} %atom_in_ref.1) | copy-start | bytes 98308
  5.4 6.5 %copy-start.5 = (bf16[1,1,32,64]{3,2,1,0:T(8,128)(2,1)S(1)}, bf16[1,1,32,64]{3,2,1,0:T(8,128)(2,1)}, u32[]{:S(2)}) copy-start(bf16[1,1,32,64]{3,2,1,0:T(8,128)(2,1)} %atom_ref.1) | copy-start | bytes 12292
  5.5 6.5 %copy-start.6 = (bf16[64,64]{1,0:T(8,128)(2,1)S(1)}, bf16[64,64]{1,0:T(8,128)(2,1)}, u32[]{:S(2)}) copy-start(bf16[64,64]{1,0:T(8,128)(2,1)} %bond_mix_ref.1) | copy-start | bytes 24580
  5.5 6.5 %copy-start.7 = (bf16[64,128]{1,0:T(8,128)(2,1)S(1)}, bf16[64,128]{1,0:T(8,128)(2,1)}, u32[]{:S(2)}) copy-start(bf16[64,128]{1,0:T(8,128)(2,1)} %angle_ref.1) | copy-start | bytes 49156
  5.5 6.5 %copy-start.8 = (bf16[64,128]{1,0:T(8,128)(2,1)S(1)}, bf16[64,128]{1,0:T(8,128)(2,1)}, u32[]{:S(2)}) copy-start(bf16[64,128]{1,0:T(8,128)(2,1)} %pair_hidden_ref.1) | copy-start | bytes 49156
  5.5 6.5 %copy-start.9 = (bf16[64,64]{1,0:T(8,128)(2,1)S(1)}, bf16[64,64]{1,0:T(8,128)(2,1)}, u32[]{:S(2)}) copy-start(bf16[64,64]{1,0:T(8,128)(2,1)} %pair_out_ref.1) | copy-start | bytes 24580
  5.5 6.5 %copy-start.10 = (bf16[64,64]{1,0:T(8,128)(2,1)S(1)}, bf16[64,64]{1,0:T(8,128)(2,1)}, u32[]{:S(2)}) copy-start(bf16[64,64]{1,0:T(8,128)(2,1)} %atom_out_ref.1) | copy-start | bytes 24580
  6.2 5.8 %copy-start.2 = (bf16[64,256]{1,0:T(8,128)(2,1)S(1)}, bf16[64,256]{1,0:T(8,128)(2,1)}, u32[]{:S(2)}) copy-start(bf16[64,256]{1,0:T(8,128)(2,1)} %pair_ref.1) | copy-start | bytes 98308
  6.2 5.8 %copy-start = (bf16[1,1,32,1024]{3,2,1,0:T(8,128)(2,1)S(1)}, bf16[1,1,32,1024]{3,2,1,0:T(8,128)(2,1)}, u32[]{:S(2)}) copy-start(bf16[1,1,32,1024]{3,2,1,0:T(8,128)(2,1)} %bond_ref.1) | copy-start | bytes 196612
  6.2 5.8 %copy-start.1 = (bf16[192,128]{1,0:T(8,128)(2,1)S(1)}, bf16[192,128]{1,0:T(8,128)(2,1)}, u32[]{:S(2)}) copy-start(bf16[192,128]{1,0:T(8,128)(2,1)} %bond_in_ref.1) | copy-start | bytes 147460
  6.3 5.7 %copy-start.4 = (s32[1,1,32,16]{2,3,1,0:T(8,128)S(1)}, s32[1,1,32,16]{2,3,1,0:T(8,128)}, u32[]{:S(2)}) copy-start(s32[1,1,32,16]{2,3,1,0:T(8,128)} %param.14) | copy-start | bytes 6148
  6.3 7.5 %collective-permute-start.3 = (bf16[144,128]{1,0:T(8,128)(2,1)S(1)}, bf16[144,128]{1,0:T(8,128)(2,1)S(1)}, u32[]{:S(2)}, u32[]{:S(2)}) collective-permute-start(bf16[144,128]{1,0:T(8,128)(2,1)S(1)} %get-tuple-element.42), channel_id=1, source_target_pairs={{0,1},{1,2},{2,3},{3,4},{4,5},{5,6},{6,7},{7,0},{8,9},{9,10},{10,1... | collective-permute-start | bytes 110600 | tf_op jit(solution)/shard_map/ppermute | solution.py:451
  8.8 5.0 %collective-permute-start.2 = (bf16[144,128]{1,0:T(8,128)(2,1)S(1)}, bf16[144,128]{1,0:T(8,128)(2,1)S(1)}, u32[]{:S(2)}, u32[]{:S(2)}) collective-permute-start(bf16[144,128]{1,0:T(8,128)(2,1)S(1)} %get-tuple-element.43), channel_id=1, source_target_pairs={{1,0},{2,1},{3,2},{4,3},{5,4},{6,5},{7,6},{0,7},{9,8},{10,9},{11,1... | collective-permute-start | bytes 110600 | tf_op jit(solution)/shard_map/ppermute | solution.py:452

commit v2 on v1

--- a/solution.py
+++ b/solution.py
@@ -136,8 +136,10 @@
         ref[row_count:] = atom
 
 
-def basis_kernel(atoms, dirs_ref, basis_ref):
-    slots, degrees, bonds = basis_ref.shape
+def basis_kernel(atoms, dirs_ref, angle_ref, angular_ref):
+    slots, _, bonds = angular_ref.shape
+    degrees = angle_ref.shape[0]
+    weight = (angle_ref[...].astype(F32) * 0.5).T.astype(BF16)
     angles = dirs_ref[...]
     sines = jnp.sin(angles)
     cosines = jnp.cos(angles)
@@ -168,7 +170,8 @@
         blocks = [lower, upper]
         for _ in range(degrees // 8 - 1):
             blocks.append(double * blocks[-1] - blocks[-2])
-        basis_ref[diagonal] = jnp.concatenate(blocks[1:], axis=0).astype(BF16)
+        basis = jnp.concatenate(blocks[1:], axis=0).astype(BF16)
+        angular_ref[diagonal] = jnp.dot(weight, basis, preferred_element_type=F32).astype(BF16)
 
 
 def prepare_kernel(
@@ -180,7 +183,6 @@
     bond_in_ref,
     bond_mix_ref,
     pair_ref,
-    angle_ref,
     pair_hidden_ref,
     pair_out_ref,
     atom_in_ref,
@@ -193,7 +195,6 @@
     far_weight_ref,
     mix_weight_ref,
     pair_weight_ref,
-    angle_weight_ref,
     hidden_weight_ref,
     out_weight_ref,
     atom_in_weight_ref,
@@ -258,16 +259,17 @@
     )
     mix_weight_ref[...] = turned(mix, 0.5)
     pair_weight_ref[...] = turned(pair_ref[...].astype(F32), 0.5)
-    angle_weight_ref[...] = turned(angle_ref[...].astype(F32), 0.5)
     hidden_weight_ref[...] = turned(pair_hidden_ref[...].astype(F32), 0.25)
-    out_weight_ref[...] = turned(pair_out_ref[...].astype(F32), 0.5)
+    out_weight = turned(pair_out_ref[...].astype(F32), 0.5)
+    out_weight_ref[...] = jnp.concatenate([out_weight] * (slots * atoms // 128), axis=1)
     atom_in_weight_ref[...] = turned(atom_in_ref[...].astype(F32), 0.5)
     atom_out_weight_ref[...] = turned(atom_out_ref[...].astype(F32), 0.5)
 
 
 def doubled_gate(values):
     half = values.shape[0] // 2
-    return values[:half] * (1.0 + jnp.tanh(values[:half])) * (1.0 + jnp.tanh(values[half:]))
+    one = jnp.ones((), values.dtype)
+    return values[:half] * (one + jnp.tanh(values[:half])) * (one + jnp.tanh(values[half:]))
 
 
 def main_kernel(
@@ -276,7 +278,7 @@
     two_ref,
     four_ref,
     three_ref,
-    basis_ref,
+    angular_ref,
     chosen_bond_ref,
     chosen_atom_ref,
     right_half_ref,
@@ -285,7 +287,6 @@
     far_weight_ref,
     mix_weight_ref,
     pair_weight_ref,
-    angle_weight_ref,
     hidden_weight_ref,
     out_weight_ref,
     atom_in_weight_ref,
@@ -295,7 +296,7 @@
     first_ref,
     second_ref,
 ):
-    slots, degrees, bonds = basis_ref.shape
+    slots, _, bonds = angular_ref.shape
     atoms = bonds // slots
     feature = values_ref.shape[0] // 2
     half = CAP // 2
@@ -326,40 +327,38 @@
     ahead = (values_ref[feature:].astype(F32) + mixed[:feature]).astype(BF16).astype(F32)
     back = (far_bond + mixed[feature:]).astype(BF16).astype(F32)
     average = ((ahead + back) * 0.5).astype(BF16)
-    projected = jnp.dot(pair_weight_ref[...], average, preferred_element_type=F32)
-    first_ref[...] = projected[: 2 * feature]
-    second = projected[2 * feature :]
-    per_group = 128 // atoms
-    for turn in range(per_group):
-        second_ref[turn] = second if turn == 0 else pltpu.roll(second, bonds - atoms * turn, 1)
+    first_ref[...] = jnp.dot(
+        pair_weight_ref[: 2 * feature], average, preferred_element_type=F32
+    ).astype(BF16)
     width = 256
     blocks = bonds // 128
-    angle_weight = angle_weight_ref[...]
     hidden_weight = hidden_weight_ref[...]
-    totals = []
-    for start in range(0, bonds, width):
-        total = jnp.zeros((feature, width), F32)
-        for diagonal in range(slots):
-            turn, skip = diagonal % per_group, diagonal // per_group
-            pieces = [
-                second_ref[turn, :, pl.ds(128 * ((start // 128 + k + skip) % blocks), 128)]
-                for k in range(width // 128)
-            ]
-            mixture = jnp.dot(
-                angle_weight,
-                basis_ref[diagonal, :, pl.ds(start, width)],
-                preferred_element_type=F32,
+    totals = [average.astype(F32)[:, start : start + width] for start in range(0, bonds, width)]
+    for turn in range(128 // atoms):
+        turned = average.astype(F32)
+        if turn > 0:
+            turned = pltpu.roll(turned, bonds - atoms * turn, 1)
+        second_ref[turn] = jnp.dot(
+            pair_weight_ref[2 * feature :], turned.astype(BF16), preferred_element_type=F32
+        ).astype(BF16)
+        for part, start in enumerate(range(0, bonds, width)):
+            gates = []
+            for skip in range(blocks):
+                pieces = [
+                    second_ref[turn, :, pl.ds((start + 128 * (k + skip)) % bonds, 128)]
+                    for k in range(width // 128)
+                ]
+                mixture = angular_ref[skip * (128 // atoms) + turn, :, pl.ds(start, width)] + (
+                    first_ref[:, pl.ds(start, width)] + jnp.concatenate(pieces, axis=1)
+                )
+                second = jnp.dot(
+                    hidden_weight, doubled_gate(mixture), preferred_element_type=F32
+                )
+                gates.append(doubled_gate(second.astype(BF16)))
+            totals[part] = totals[part] + jnp.dot(
+                out_weight_ref[...], jnp.concatenate(gates, axis=0), preferred_element_type=F32
             )
-            mixture = mixture + (first_ref[:, pl.ds(start, width)] + jnp.concatenate(pieces, axis=1))
-            pair = doubled_gate(mixture).astype(BF16)
-            total = total + doubled_gate(
-                jnp.dot(hidden_weight, pair, preferred_element_type=F32)
-            )
-        totals.append(total)
-    pair_sum = jnp.concatenate(totals, axis=1).astype(BF16)
-    bond_out = (
-        average.astype(F32) + jnp.dot(out_weight_ref[...], pair_sum, preferred_element_type=F32)
-    ).astype(BF16).astype(F32)
+    bond_out = jnp.concatenate(totals, axis=1).astype(BF16).astype(F32)
     rows = bond_out.T.astype(BF16)
     for slot in range(slots):
         bond_result_ref[0, 0, :, slot * feature : (slot + 1) * feature] = rows[
@@ -401,7 +400,6 @@
     atoms, feature = atom_feat.shape[2], atom_feat.shape[3]
     slots = neighbours.shape[3]
     bonds = atoms * slots
-    degrees = angle_weight.shape[0]
     extents = (lax.axis_size("gx"), lax.axis_size("gy"))
     targets = neighbours[0, 0].T
     dirs = bond_dirs[:, 0, 0].reshape(2, atoms, slots).transpose(0, 2, 1).reshape(2, bonds)
@@ -432,16 +430,18 @@
     first, second = moves(extents[0], paired[0])
     one = lax.ppermute(one, "gx", first)
     two = lax.ppermute(two, "gx", second)
-    basis = pl.pallas_call(
+    angular = pl.pallas_call(
         functools.partial(basis_kernel, atoms),
-        out_shape=shaped((slots, degrees, bonds), BF16),
-        in_specs=[vmem],
+        out_shape=shaped((slots, 2 * feature, bonds), BF16),
+        in_specs=[vmem, vmem],
         out_specs=vmem,
         compiler_params=params,
-        cost_estimate=pl.CostEstimate(flops=4 * 2**20, bytes_accessed=2**20, transcendentals=4096),
-        name="basis",
-    )(dirs)
-    own, one, two, basis = lax.optimization_barrier((own, one, two, basis))
+        cost_estimate=pl.CostEstimate(
+            flops=128 * 2**20, bytes_accessed=2**21, transcendentals=4096
+        ),
+        name="angular",
+    )(dirs, angle_weight)
+    own, one, two, angular = lax.optimization_barrier((own, one, two, angular))
     first, second = moves(extents[1], paired[1])
 
     def forwarded(block):
@@ -454,9 +454,8 @@
         shaped((4 * feature, 2 * feature), BF16),
         shaped((2 * feature, 2 * feature), BF16),
         shaped((4 * feature, feature), BF16),
-        shaped((2 * feature, degrees), BF16),
         shaped((2 * feature, feature), BF16),
-        shaped((feature, feature), BF16),
+        shaped((feature, feature * (bonds // 128)), BF16),
         shaped((2 * feature, 2 * feature), BF16),
         shaped((feature, feature), BF16),
     )
@@ -470,8 +469,8 @@
             shaped((4 * feature, bonds), F32),
         )
         + weights,
-        in_specs=[vmem] * 11,
-        out_specs=(vmem,) * 13,
+        in_specs=[vmem] * 10,
+        out_specs=(vmem,) * 12,
         compiler_params=params,
         cost_estimate=pl.CostEstimate(flops=64 * 2**20, bytes_accessed=2**21, transcendentals=0),
         name="prepare",
@@ -482,7 +481,6 @@
         bond_in_weight,
         bond_mix_weight,
         pair_weight,
-        angle_weight,
         pair_hidden_weight,
         pair_out_weight,
         atom_in_weight,
@@ -491,18 +489,18 @@
     return pl.pallas_call(
         main_kernel,
         out_shape=(shaped(atom_feat.shape, BF16), shaped(bond_feat.shape, BF16)),
-        in_specs=[vmem] * 19,
+        in_specs=[vmem] * 18,
         out_specs=(vmem, vmem),
         scratch_shapes=[
-            pltpu.VMEM((2 * feature, bonds), F32),
-            pltpu.VMEM((128 // atoms, 2 * feature, bonds), F32),
+            pltpu.VMEM((2 * feature, bonds), BF16),
+            pltpu.VMEM((128 // atoms, 2 * feature, bonds), BF16),
         ],
         compiler_params=params,
         cost_estimate=pl.CostEstimate(
             flops=400 * 2**20, bytes_accessed=2**22, transcendentals=2**21
         ),
         name="main",
-    )(own, one, two, four, three, basis, *prepared)
+    )(own, one, two, four, three, angular, *prepared)
 
 
 def solution(mesh):

time: 17.6 us -> 19.4 us (1.10)
  Pallas kernels: 6.4 us -> 7.76 us
  starting transfers between devices: 8.74 us -> 7.9 us
  local copies, waits for them, and re-layouts: 0.35 us -> 1.05 us
  other arithmetic: 0.02 us -> 0.71 us
    ppermute x1, starting transfers between devices: 2.5 us -> 1.57 us  [per_device(): three = lax.ppermute(forwarded(1), 'gy', first)]
    pallas_call x1, Pallas kernels: 3.63 us -> 4.53 us  [per_device(): pl.pallas_call(main_kernel, out_shape=(shaped(atom_feat.shape, BF16), sha...]
    unnamed x29 -> x27, local copies, waits for them, and re-layouts: 0.1 us -> 0.81 us
    unnamed x1, other arithmetic: 0.02 us -> 0.71 us
    pallas_call x1, Pallas kernels: 0.49 us -> 0.84 us  [per_device(): pl.pallas_call(functools.partial(basis_kernel, atoms), out_shape=shaped((...]
  transfers between devices with their start and end apart: 4 -> 4, of which waited for: 2 -> 1; matrix products, arithmetic and copies ran while one was open for 1% -> 5% of each run, Pallas kernels for 8% -> 9%
where the time goes in v2:
time: 19.4 us; the launch traced here: 19.2 us
  starting transfers between devices  7.9 us (41%)
  Pallas kernels  7.76 us (40%)
  local copies, waits for them, and re-layouts  1.05 us (5%)
  waiting for transfers between devices  0.93 us (5%)
  between operations  0.8 us (4%)
  other arithmetic  0.71 us (4%)
    pallas_call x1, Pallas kernels, per_device(): pl.pallas_call(main_kernel, out_shape=(shaped(atom_feat.shape, BF16), sha...  4.53 us
    ppermute x1, starting transfers between devices, per_device(): four = lax.ppermute(forwarded(2), 'gy', second)  3.2 us
    ppermute x1, starting transfers between devices, per_device(): one = lax.ppermute(one, 'gx', first)  2.45 us
    ppermute x1, starting transfers between devices, per_device(): three = lax.ppermute(forwarded(1), 'gy', first)  1.57 us
    pallas_call x1, Pallas kernels, per_device(): pl.pallas_call(functools.partial(pack_kernel, extents, paired), out_shape...  1.47 us
    ppermute x1, waiting for transfers between devices, per_device(): three = lax.ppermute(forwarded(1), 'gy', first)  0.93 us
    pallas_call x1, Pallas kernels, per_device(): pl.pallas_call(functools.partial(prepare_kernel, extents, paired), out_sh...  0.92 us
    pallas_call x1, Pallas kernels, per_device(): pl.pallas_call(functools.partial(basis_kernel, atoms), out_shape=shaped((...  0.84 us
  transfers between devices with their start and end apart: 4, of which 1 were waited for; matrix products, arithmetic and copies ran while one was open for 5% of the time, Pallas kernels for 9%

profile of v2, /device:TPU:0, one launch (start us, length us, event | category | flops | bytes accessed | tf_op | source)
XLA Modules:
  0.0 19.2 jit_solution(12528322668200604259)
XLA Ops:
  0.6 0.0 copy-start
  0.6 0.0 copy-start.3
  0.7 0.0 copy-start.2
  0.7 0.0 copy-start.5
  0.7 0.0 copy-start.4
  0.7 0.0 copy-start.1
  0.7 1.5 %pack.1 = (bf16[112,128]{1,0:T(8,128)(2,1)S(1)}, bf16[112,128]{1,0:T(8,128)(2,1)S(1)}, bf16[112,128]{1,0:T(8,128)(2,1)S(1)}) custom-call(s32[16,32]{1,0:T(8,128)} %bitcast.4, bf16[1,1,32,64]{3,2,1,0:T(8,128)(2,1)} %atom_ref.1, bf16[1,1,32,1024]{3,2,1,0:T(8,128)(2,1)} %bond_ref.1), custom_call_target="tpu_custom_call" | custom-call | tf_op jit(solution)/shard_map/pack/pallas_call | solution.py:416
  2.2 2.4 %collective-permute-start = (bf16[112,128]{1,0:T(8,128)(2,1)S(1)}, bf16[112,128]{1,0:T(8,128)(2,1)S(1)}, u32[]{:S(2)}, u32[]{:S(2)}) collective-permute-start(bf16[112,128]{1,0:T(8,128)(2,1)S(1)} %get-tuple-element.22), channel_id=1, source_target_pairs={{0,24},{8,16},{16,8},{24,0},{1,25},{9,17},{17,9},{25,1},{2,26},{10... | collective-permute-start | bytes 86024 | tf_op jit(solution)/shard_map/ppermute | solution.py:431
  4.6 0.7 %collective-permute-start.1 = (bf16[112,128]{1,0:T(8,128)(2,1)S(1)}, bf16[112,128]{1,0:T(8,128)(2,1)S(1)}, u32[]{:S(2)}, u32[]{:S(2)}) collective-permute-start(bf16[112,128]{1,0:T(8,128)(2,1)S(1)} %get-tuple-element.23), channel_id=1, source_target_pairs={{0,8},{8,0},{16,24},{24,16},{1,9},{9,1},{17,25},{25,17},{2,10},{10... | collective-permute-start | bytes 86024 | tf_op jit(solution)/shard_map/ppermute | solution.py:432
  5.3 0.7 %reduce = f32[2,512]{1,0:T(2,128)S(1)} reduce(f32[2,1,1,512]{3,2,1,0:T(1,128)} %param.15, f32[]{:T(128)} %constant.4), dimensions={1,2}, to_apply=%param.15.reduce_sub_computation | reduce | bytes 8196 | tf_op args[3]
  6.0 0.1 reshape_squeeze.3
  6.1 0.1 copy.15
  6.2 0.1 reshape.7.dirs_ref
  6.2 0.0 copy-start.6
  6.2 0.7 %copy-done.6 = bf16[64,128]{1,0:T(8,128)(2,1)S(1)} copy-done((bf16[64,128]{1,0:T(8,128)(2,1)S(1)}, bf16[64,128]{1,0:T(8,128)(2,1)}, u32[]{:S(2)}) %copy-start.6) | copy-done | bytes 16408
  7.0 0.0 copy-start.7
  7.0 0.0 copy-start.8
  7.0 0.0 copy-start.9
  7.0 0.0 copy-start.10
  7.0 0.8 %angular.1.angular_ref = bf16[16,128,512]{2,1,0:T(8,128)(2,1)S(1)} custom-call(f32[2,512]{1,0:T(2,128)S(1)} %reshape.7.dirs_ref, bf16[64,128]{1,0:T(8,128)(2,1)S(1)} %copy-done.6), custom_call_target="tpu_custom_call" | custom-call | flops 134217728 | bytes 2097152 | tf_op jit(solution)/shard_map/angular/pallas_call | solution.py:433
  7.8 0.0 collective-permute-done.one_ref
  7.8 0.0 collective-permute-done.1.two_ref
  7.9 1.6 %collective-permute-start.3 = (bf16[144,128]{1,0:T(8,128)(2,1)S(1)}, bf16[144,128]{1,0:T(8,128)(2,1)S(1)}, u32[]{:S(2)}, u32[]{:S(2)}) collective-permute-start(bf16[144,128]{1,0:T(8,128)(2,1)S(1)} %get-tuple-element.40), channel_id=1, source_target_pairs={{0,1},{1,2},{2,3},{3,4},{4,5},{5,6},{6,7},{7,0},{8,9},{9,10},{10,1... | collective-permute-start | bytes 110600 | tf_op jit(solution)/shard_map/ppermute | solution.py:451
  9.5 3.2 %collective-permute-start.2 = (bf16[144,128]{1,0:T(8,128)(2,1)S(1)}, bf16[144,128]{1,0:T(8,128)(2,1)S(1)}, u32[]{:S(2)}, u32[]{:S(2)}) collective-permute-start(bf16[144,128]{1,0:T(8,128)(2,1)S(1)} %get-tuple-element.41), channel_id=1, source_target_pairs={{1,0},{2,1},{3,2},{4,3},{5,4},{6,5},{7,6},{0,7},{9,8},{10,9},{11,1... | collective-permute-start | bytes 110600 | tf_op jit(solution)/shard_map/ppermute | solution.py:452
  12.7 0.0 copy-done
  12.7 0.0 copy-done.3
  12.7 0.0 copy-done.2
  12.7 0.0 copy-done.5
  12.7 0.0 copy-done.4
  12.7 0.0 copy-done.1
  12.7 0.0 copy-done.7
  12.7 0.0 copy-done.8
  12.7 0.0 copy-done.9
  12.8 0.0 copy-done.10
  12.8 0.9 %prepare.1 = (bf16[288,512]{1,0:T(8,128)(2,1)S(1)}, bf16[144,512]{1,0:T(8,128)(2,1)S(1)}, f32[8,512]{1,0:T(8,128)S(1)}, bf16[128,512]{1,0:T(8,128)(2,1)S(1)}, f3...) custom-call(s32[16,32]{1,0:T(8,128)S(1)} %bitcast.5, ...), custom_call_target="tpu_custom_call" | custom-call | flops 67108864 | bytes 2097152 | tf_op jit(solution)/shard_map/prepare/pallas_call | solution.py:462
  13.7 0.9 %collective-permute-done.3.three_ref = bf16[144,128]{1,0:T(8,128)(2,1)S(1)} collective-permute-done((bf16[144,128]{1,0:T(8,128)(2,1)S(1)}, bf16[144,128]{1,0:T(8,128)(2,1)S(1)}, u32[]{:S(2)}, u32[]{:S(2)}) %collective-permute-start.3) | collective-permute-done | bytes 36896 | tf_op jit(solution)/shard_map/ppermute | solution.py:451
  14.6 0.0 collective-permute-done.2.four_ref
  14.6 4.5 %main.1 = (bf16[1,1,32,64]{3,2,1,0:T(8,128)(2,1)}, bf16[1,1,32,1024]{3,2,1,0:T(8,128)(2,1)}) custom-call(bf16[112,128]{1,0:T(8,128)(2,1)S(1)} %get-tuple-element.24.own_ref, bf16[112,128]{1,0:T(8,128)(2,1)S(1)} %collective-permute-done.one_ref, bf16[112,128]{1,0:T(8,128)(2,1)S(1)} %collective-permute-done.1.two_ref, ...), custom_call_target="tpu_custom_call" | custom-call | flops 419430400 | bytes 4194304 | tf_op jit(solution)/shard_map/main/pallas_call | solution.py:489
  (6 shorter events, 0.1 us)
Async XLA Ops:
  0.6 12.1 %copy-start = (bf16[1,1,32,1024]{3,2,1,0:T(8,128)(2,1)S(1)}, bf16[1,1,32,1024]{3,2,1,0:T(8,128)(2,1)}, u32[]{:S(2)}) copy-start(bf16[1,1,32,1024]{3,2,1,0:T(8,128)(2,1)} %bond_ref.1) | copy-start | bytes 196612
  0.6 12.1 %copy-start.3 = (bf16[1,1,32,64]{3,2,1,0:T(8,128)(2,1)S(1)}, bf16[1,1,32,64]{3,2,1,0:T(8,128)(2,1)}, u32[]{:S(2)}) copy-start(bf16[1,1,32,64]{3,2,1,0:T(8,128)(2,1)} %atom_ref.1) | copy-start | bytes 12292
  0.7 12.1 %copy-start.2 = (s32[1,1,32,16]{2,3,1,0:T(8,128)S(1)}, s32[1,1,32,16]{2,3,1,0:T(8,128)}, u32[]{:S(2)}) copy-start(s32[1,1,32,16]{2,3,1,0:T(8,128)} %param.14) | copy-start | bytes 6148
  0.7 12.0 %copy-start.5 = (bf16[128,128]{1,0:T(8,128)(2,1)S(1)}, bf16[128,128]{1,0:T(8,128)(2,1)}, u32[]{:S(2)}) copy-start(bf16[128,128]{1,0:T(8,128)(2,1)} %atom_in_ref.1) | copy-start | bytes 98308
  0.7 12.0 %copy-start.4 = (bf16[64,256]{1,0:T(8,128)(2,1)S(1)}, bf16[64,256]{1,0:T(8,128)(2,1)}, u32[]{:S(2)}) copy-start(bf16[64,256]{1,0:T(8,128)(2,1)} %pair_ref.1) | copy-start | bytes 98308
  0.7 12.0 %copy-start.1 = (bf16[192,128]{1,0:T(8,128)(2,1)S(1)}, bf16[192,128]{1,0:T(8,128)(2,1)}, u32[]{:S(2)}) copy-start(bf16[192,128]{1,0:T(8,128)(2,1)} %bond_in_ref.1) | copy-start | bytes 147460
  2.2 5.7 %collective-permute-start = (bf16[112,128]{1,0:T(8,128)(2,1)S(1)}, bf16[112,128]{1,0:T(8,128)(2,1)S(1)}, u32[]{:S(2)}, u32[]{:S(2)}) collective-permute-start(bf16[112,128]{1,0:T(8,128)(2,1)S(1)} %get-tuple-element.22), channel_id=1, source_target_pairs={{0,24},{8,16},{16,8},{24,0},{1,25},{9,17},{17,9},{25,1},{2,26},{10... | collective-permute-start | bytes 86024 | tf_op jit(solution)/shard_map/ppermute | solution.py:431
  4.6 3.2 %collective-permute-start.1 = (bf16[112,128]{1,0:T(8,128)(2,1)S(1)}, bf16[112,128]{1,0:T(8,128)(2,1)S(1)}, u32[]{:S(2)}, u32[]{:S(2)}) collective-permute-start(bf16[112,128]{1,0:T(8,128)(2,1)S(1)} %get-tuple-element.23), channel_id=1, source_target_pairs={{0,8},{8,0},{16,24},{24,16},{1,9},{9,1},{17,25},{25,17},{2,10},{10... | collective-permute-start | bytes 86024 | tf_op jit(solution)/shard_map/ppermute | solution.py:432
  6.2 0.7 %copy-start.6 = (bf16[64,128]{1,0:T(8,128)(2,1)S(1)}, bf16[64,128]{1,0:T(8,128)(2,1)}, u32[]{:S(2)}) copy-start(bf16[64,128]{1,0:T(8,128)(2,1)} %angle_ref.1) | copy-start | bytes 49156
  7.0 5.8 %copy-start.7 = (bf16[64,64]{1,0:T(8,128)(2,1)S(1)}, bf16[64,64]{1,0:T(8,128)(2,1)}, u32[]{:S(2)}) copy-start(bf16[64,64]{1,0:T(8,128)(2,1)} %bond_mix_ref.1) | copy-start | bytes 24580
  7.0 5.8 %copy-start.8 = (bf16[64,128]{1,0:T(8,128)(2,1)S(1)}, bf16[64,128]{1,0:T(8,128)(2,1)}, u32[]{:S(2)}) copy-start(bf16[64,128]{1,0:T(8,128)(2,1)} %pair_hidden_ref.1) | copy-start | bytes 49156
  7.0 5.8 %copy-start.9 = (bf16[64,64]{1,0:T(8,128)(2,1)S(1)}, bf16[64,64]{1,0:T(8,128)(2,1)}, u32[]{:S(2)}) copy-start(bf16[64,64]{1,0:T(8,128)(2,1)} %pair_out_ref.1) | copy-start | bytes 24580
  7.0 5.8 %copy-start.10 = (bf16[64,64]{1,0:T(8,128)(2,1)S(1)}, bf16[64,64]{1,0:T(8,128)(2,1)}, u32[]{:S(2)}) copy-start(bf16[64,64]{1,0:T(8,128)(2,1)} %atom_out_ref.1) | copy-start | bytes 24580
  7.9 6.7 %collective-permute-start.3 = (bf16[144,128]{1,0:T(8,128)(2,1)S(1)}, bf16[144,128]{1,0:T(8,128)(2,1)S(1)}, u32[]{:S(2)}, u32[]{:S(2)}) collective-permute-start(bf16[144,128]{1,0:T(8,128)(2,1)S(1)} %get-tuple-element.40), channel_id=1, source_target_pairs={{0,1},{1,2},{2,3},{3,4},{4,5},{5,6},{6,7},{7,0},{8,9},{9,10},{10,1... | collective-permute-start | bytes 110600 | tf_op jit(solution)/shard_map/ppermute | solution.py:451
  9.5 5.1 %collective-permute-start.2 = (bf16[144,128]{1,0:T(8,128)(2,1)S(1)}, bf16[144,128]{1,0:T(8,128)(2,1)S(1)}, u32[]{:S(2)}, u32[]{:S(2)}) collective-permute-start(bf16[144,128]{1,0:T(8,128)(2,1)S(1)} %get-tuple-element.41), channel_id=1, source_target_pairs={{1,0},{2,1},{3,2},{4,3},{5,4},{6,5},{7,6},{0,7},{9,8},{10,9},{11,1... | collective-permute-start | bytes 110600 | tf_op jit(solution)/shard_map/ppermute | solution.py:452
